TPU v7x, 128 devices: a whole 4x4x4 slice. The times are simulated.
128 devices in a mesh: seq: 32 (over y, z_lo, x), loop: 4 (over z_hi, core).
Axes of the slice: x: 4, y: 4, z: 4 (z_hi: 2, z_lo: 2; z = z_hi * 2 + z_lo), core: 2. Of those that a mesh axis runs over, the one named last changes fastest.
Arguments:
- events: bfloat16 [4, 16384, 512], P('loop', 'seq'), may hold values from -6 to 6
- carried: float32 [4, 16384, 512], P('loop', 'seq'), may hold values from -48 to 48
- positions: int32 [4, 16384], P('loop', 'seq'), may hold values from 0 to 8192, as said below
- neg_ids: int32 [4, 32, 4096], P('loop', 'seq'), may hold values from 0 to 524287, as said below
- pos_ids: int32 [4, 16384], P('loop', 'seq'), may hold values from 0 to 524287, as said below
- in_gain: float32 [512], replicated, may hold values from 0.5 to 1.5
- w_in: bfloat16 [512, 2048], replicated, may hold values from -0.25 to 0.25
- attn_gain: float32 [512], replicated, may hold values from 0.5 to 1.5
- w_out: bfloat16 [512, 512], replicated, may hold values from -0.25 to 0.25
- table: bfloat16 [524288, 512], P(('seq', 'loop')), may hold values from -0.25 to 0.25
Outputs:
- token_losses: float32 [4, 16384], P('loop', 'seq')
- grad_hidden: bfloat16 [4, 16384, 512], P('loop', 'seq')
- grad_table: float32 [524288, 512], P(('seq', 'loop'))
Inputs may be any that keep to these rules, and one draw needn't show every extreme that they name: `positions`: nondecreasing along each history from 0 at its first event, rising by 0 or 1 from one event to the next. `neg_ids`: slot k of every block names a row held by table device k // 32, the table's rows lying in runs of 4096 over the devices in the order seq+loop. `pos_ids`: the 512 events of one block name rows of one table device at most 8 times; in every block some table device is named exactly 8 times.
All inputs are finite; a program needn't handle non-finite values.
Results may differ from a plain program's by a relative error of at most 0.005.
The roundings to bfloat16 on the way count: a program that leaves them out, or rounds other values in their place, can miss the bound.
Values may be sent and summed in bfloat16 or wider, within the bound.
A program may use at most 128 MiB of HBM per device.

v0:
```python
import jax
import jax.numpy as jnp
from jax import lax
from jax.experimental import pallas as pl
from jax.experimental.pallas import tpu as pltpu
from jax.sharding import PartitionSpec as P

HEADS = 8
DH = 64
WINDOW = 4
WIDTH = HEADS * DH
LANES = 128
BANDS = WIDTH // LANES
TOKENS = 512
NEG = 4096
ROWS = 4096
DEVICES = 128
PER_OWNER = NEG // DEVICES
CAPACITY = 2 * TOKENS // DEVICES
ASKED = PER_OWNER + CAPACITY
MESSAGE = ASKED * BANDS
GROUP = 16
GROUPS = DEVICES // GROUP
GROUP_NEG = GROUP * PER_OWNER
GROUP_POS = GROUP * CAPACITY
NEG_LINES = PER_OWNER * BANDS

SHARPNESS = 50.0
LOG2E = 1.4426950408889634
EPSILON = 1e-06
F32 = jnp.float32
BF16 = jnp.bfloat16
NT = (((1,), (1,)), ((), ()))
TN = (((0,), (0,)), ((), ()))
BANK = 62 * 2**20


def silu(value):
    half = value * 0.5
    return half + half * jnp.tanh(half)


def row_sum(value):
    return jnp.sum(value, axis=-1, keepdims=True)


def normalise(rows, gain):
    wide = rows.astype(F32)
    scale = lax.rsqrt(row_sum(wide * wide) * (1.0 / WIDTH) + EPSILON)
    return (wide * scale * gain).astype(BF16)


def store_bands(ref, lead, value):
    for band in range(BANDS):
        ref[lead + (band,)] = value[:, band * LANES : (band + 1) * LANES]


def project_own(events, gain, w_in, gate, queries, keys, values):
    normed = normalise(events[...], gain[...])

    def column(index):
        part = jnp.dot(
            normed, w_in[:, index * WIDTH : (index + 1) * WIDTH], preferred_element_type=F32
        )
        return silu(part).astype(BF16)

    gate[...] = column(0)
    store_bands(values, (0,), column(1))
    store_bands(queries, (), (column(2).astype(F32) * 0.0625).astype(BF16))
    store_bands(keys, (0,), column(3))


def project_far(reach, rows, live, gain, w_in, keys, values):
    normed = normalise(rows, gain[...])

    def column(index):
        part = jnp.dot(
            normed, w_in[:, index * WIDTH : (index + 1) * WIDTH], preferred_element_type=F32
        )
        return (silu(part) * live).astype(BF16)

    store_bands(values, (reach,), column(1))
    store_bands(keys, (reach,), column(3))


def attend(stamp_cols, stamp_row, queries, keys, values, mixed):
    allowed = stamp_row[...] <= stamp_cols[:, :1]
    first = lax.broadcasted_iota(jnp.int32, (TOKENS, LANES), 1) < DH

    def pair(band, _):
        both = queries[band].astype(F32)
        parts = [
            jnp.where(first, both, 0.0).astype(BF16),
            jnp.where(first, 0.0, both).astype(BF16),
        ]

        def block(index, own):
            outs = []
            for part in parts:
                half = lax.dot_general(part, keys[index, band], NT, preferred_element_type=F32)
                weight = half + half * jnp.tanh(half)
                if own:
                    weight = jnp.where(allowed, weight, 0.0)
                outs.append(
                    jnp.dot(weight.astype(BF16), values[index, band], preferred_element_type=F32)
                )
            return jnp.where(first, outs[0], outs[1])

        mixed[band] = block(0, True)

        def later(index, _):
            mixed[band] += block(index, False)
            return 0

        lax.fori_loop(1, WINDOW, later, 0)
        return 0

    lax.fori_loop(0, BANDS, pair, 0)


def finish_hidden(events, carried, gain, w_out, gate, mixed, hidden):
    parts = [
        carried[:, band * LANES : (band + 1) * LANES] + mixed[band] for band in range(BANDS)
    ]
    squares = sum(row_sum(part * part) for part in parts)
    scale = lax.rsqrt(squares * (1.0 / WIDTH) + EPSILON)
    attended = jnp.concatenate(parts, axis=1)
    gated = (attended * scale * gain[...] * gate[...].astype(F32)).astype(BF16)
    hidden[...] = (
        events[...].astype(F32) + jnp.dot(gated, w_out[...], preferred_element_type=F32)
    ).astype(BF16)


def widen_table(table, lines):
    step = 256

    def part(index, _):
        start = pl.multiple_of(index * step, step)
        rows = table[pl.ds(start, step), :].astype(F32)
        for band in range(BANDS):
            lines[pl.ds(start * BANDS + band, step, stride=BANDS), :] = rows[
                :, band * LANES : (band + 1) * LANES
            ]
        return 0

    lax.fori_loop(0, ROWS // step, part, 0)


def answer(asked, lines, stage, message, peer):
    for slot in range(ASKED):
        row = jnp.maximum(asked[peer, slot], 0)
        stage[pl.ds(slot * BANDS, BANDS), :] = lines[pl.ds(row * BANDS, BANDS), :]
    for band in range(BANDS):
        message[peer, pl.ds(band * PER_OWNER, PER_OWNER), :] = stage[
            pl.ds(band, PER_OWNER, stride=BANDS), :
        ].astype(BF16)
    tail = [
        stage[pl.ds(NEG_LINES + band, CAPACITY, stride=BANDS), :] for band in range(BANDS)
    ]
    message[peer, pl.ds(NEG_LINES, CAPACITY * BANDS), :] = jnp.concatenate(tail, axis=0).astype(
        BF16
    )


def neg_rows(message, group):
    start = pl.multiple_of(group * GROUP, GROUP)
    parts = [
        message[pl.ds(start, GROUP), pl.ds(band * PER_OWNER, PER_OWNER), :].reshape(
            GROUP_NEG, LANES
        )
        for band in range(BANDS)
    ]
    return jnp.concatenate(parts, axis=1)


def pos_rows(message, group):
    start = pl.multiple_of(group * GROUP, GROUP)
    block = message[pl.ds(start, GROUP), pl.ds(NEG_LINES, CAPACITY * BANDS), :].astype(F32)
    block = block.reshape(GROUP, BANDS, CAPACITY, LANES)
    parts = [block[:, band].reshape(GROUP_POS, LANES) for band in range(BANDS)]
    return jnp.concatenate(parts, axis=1)


def unit_hidden(hidden, hidden_unit):
    wide = hidden[...].astype(F32)
    scale = lax.rsqrt(row_sum(wide * wide) + EPSILON)
    hidden_unit[...] = (wide * scale).astype(BF16)


def pick(slot_cols, group):
    lane = lax.broadcasted_iota(jnp.int32, (TOKENS, GROUP_POS), 1) + group * GROUP_POS
    return jnp.where(slot_cols[...] == lane, 1.0, 0.0).astype(BF16)


def share_rows(group, band):
    return pl.ds(pl.multiple_of((group * BANDS + band) * TOKENS, TOKENS), TOKENS)


def unit_rows(group):
    return pl.ds(pl.multiple_of(group * GROUP_NEG, GROUP_NEG), GROUP_NEG)


def meet_group(group, message, neg_ids, pos_cols, slot_cols, hidden_unit, units, shares, sums, targets):
    wide = neg_rows(message, group).astype(F32)
    scale = lax.rsqrt(row_sum(wide * wide) + EPSILON)
    unit = (wide * scale).astype(BF16)
    units[unit_rows(group), :] = unit
    logits = lax.dot_general(hidden_unit[...], unit, NT, preferred_element_type=F32)
    total = sums[...]
    for band in range(BANDS):
        keep = neg_ids[pl.ds(group * BANDS + band, 1), :] != pos_cols[...]
        near = logits[:, band * LANES : (band + 1) * LANES]
        grown = jnp.where(keep, jnp.exp2(near * (SHARPNESS * LOG2E)), 0.0)
        shares[share_rows(group, band), :] = grown
        total = total + grown
    sums[...] = total
    targets[...] += jnp.dot(
        pick(slot_cols, group),
        pos_rows(message, group).astype(BF16),
        preferred_element_type=F32,
    )


def settle(hidden_unit, sums, targets, loss, inverse):
    state = hidden_unit[...].astype(F32)
    wide = targets[...]
    scale = lax.rsqrt(row_sum(wide * wide) + EPSILON)
    unit = wide * scale
    logit = row_sum(state * unit) * SHARPNESS
    grown = jnp.exp(logit)
    total = grown + row_sum(sums[...])
    lost = jnp.broadcast_to(jnp.log(total) - logit, (TOKENS, LANES))
    for part in range(TOKENS // LANES):
        loss[pl.ds(part, 1), :] = lost[part * LANES : (part + 1) * LANES].T[:1]
    share = grown / total - 1.0
    inverse[...] = jnp.broadcast_to(1.0 / total, (TOKENS, LANES))
    upstream = (share * SHARPNESS) * state
    back = scale * (upstream - unit * row_sum(unit * upstream))
    targets[...] = (share * SHARPNESS) * unit
    return back.astype(BF16)


def return_group(group, message, slot_cols, hidden_unit, units, shares, inverse, d_pos, d_state, out):
    share = jnp.concatenate(
        [
            (shares[share_rows(group, band), :] * inverse[...]).astype(BF16)
            for band in range(BANDS)
        ],
        axis=1,
    )
    wide = neg_rows(message, group).astype(F32)
    scale = lax.rsqrt(row_sum(wide * wide) + EPSILON)
    unit = wide * scale
    upstream = (
        lax.dot_general(share, hidden_unit[...], TN, preferred_element_type=F32) * SHARPNESS
    )
    back = (scale * (upstream - unit * row_sum(unit * upstream))).astype(BF16)
    start = pl.multiple_of(group * GROUP, GROUP)
    for band in range(BANDS):
        out[pl.ds(start, GROUP), pl.ds(band * PER_OWNER, PER_OWNER), :] = back[
            :, band * LANES : (band + 1) * LANES
        ].reshape(GROUP, PER_OWNER, LANES)
    returned = lax.dot_general(pick(slot_cols, group), d_pos[...], TN, preferred_element_type=F32)
    parts = [
        returned[:, band * LANES : (band + 1) * LANES].reshape(GROUP, 1, CAPACITY, LANES)
        for band in range(BANDS)
    ]
    out[pl.ds(start, GROUP), pl.ds(NEG_LINES, CAPACITY * BANDS), :] = (
        jnp.concatenate(parts, axis=1).reshape(GROUP, CAPACITY * BANDS, LANES).astype(BF16)
    )
    d_state[...] += jnp.dot(share, units[unit_rows(group), :], preferred_element_type=F32)


def hidden_back(hidden, d_state, targets, grad):
    wide = hidden[...].astype(F32)
    scale = lax.rsqrt(row_sum(wide * wide) + EPSILON)
    unit = wide * scale
    upstream = d_state[...] * SHARPNESS + targets[...]
    grad[...] = (scale * (upstream - unit * row_sum(unit * upstream))).astype(BF16)


def add_group(group, message, neg_asked, pos_asked, total, done):
    negs = neg_rows(message, group)
    poss = pos_rows(message, group).astype(BF16)
    step = 512

    def tile(index, _):
        start = pl.multiple_of(index * step, step)
        row = lax.broadcasted_iota(jnp.int32, (step, LANES), 0) + start

        def hits(asked, line):
            return jnp.where(row == asked[pl.ds(line, 1), :], 1.0, 0.0).astype(BF16)

        wide = jnp.concatenate(
            [hits(neg_asked, group * BANDS + band) for band in range(BANDS)], axis=1
        )
        part = jnp.dot(wide, negs, preferred_element_type=F32)
        part += jnp.dot(hits(pos_asked, group), poss, preferred_element_type=F32)
        total[pl.ds(start, step), :] += part
        done(start, step)
        return 0

    lax.fori_loop(0, ROWS // step, tile, 0)


SEQ_BITS = ("x0", "x1", "zl", "y0", "y1")
LOOP_BITS = ("c", "zh")
ITEM_FLIPS = (("y0", "zh", "c"), ("x0", "y1"), ("zl", "c"), ("x1", "zh"))
GROUP_FLIPS = ("c", "zh", "y1")


def own_bits():
    seq, loop = lax.axis_index("seq"), lax.axis_index("loop")
    bits = {name: lax.rem(lax.div(seq, 2**at), 2) for at, name in enumerate(SEQ_BITS)}
    bits.update({name: lax.rem(lax.div(loop, 2**at), 2) for at, name in enumerate(LOOP_BITS)})
    return bits


def partners(group):
    bits = own_bits()
    for at, name in enumerate(GROUP_FLIPS):
        turn = lax.rem(lax.div(group, 2**at), 2)
        bits[name] = bits[name] + turn - 2 * bits[name] * turn
    seq = sum(bits[name] * 2**at for at, name in enumerate(SEQ_BITS))
    loop = sum(bits[name] * 2**at for at, name in enumerate(LOOP_BITS))
    seq_turn = {name: (1 - 2 * bits[name]) * 2**at for at, name in enumerate(SEQ_BITS)}
    loop_turn = {name: (1 - 2 * bits[name]) * 2**at for at, name in enumerate(LOOP_BITS)}
    met = []
    for item in range(GROUP):
        flips = set()
        for at, names in enumerate(ITEM_FLIPS):
            if item >> at & 1:
                flips ^= set(names)
        met.append(
            (
                sum((seq_turn[name] for name in SEQ_BITS if name in flips), seq),
                sum((loop_turn[name] for name in LOOP_BITS if name in flips), loop),
            )
        )
    return met


def each_partner(act):
    def one(group, _):
        for item, device in enumerate(partners(group)):
            slot = group * GROUP + item
            if item == 0:

                @pl.when(group > 0)
                def _():
                    act(slot, device)

            else:
                act(slot, device)
        return 0

    lax.fori_loop(0, GROUPS, one, 0)


def slot_of(owner):
    me = lax.axis_index("seq") * 4 + lax.axis_index("loop")
    apart = jnp.bitwise_xor(owner, me)
    names = LOOP_BITS + SEQ_BITS
    bit = {name: jnp.bitwise_and(jnp.right_shift(apart, at), 1) for at, name in enumerate(names)}
    first = jnp.bitwise_xor(jnp.bitwise_xor(bit["c"], bit["y0"]), bit["zl"])
    second = jnp.bitwise_xor(jnp.bitwise_xor(bit["zh"], bit["y0"]), bit["x1"])
    third = jnp.bitwise_xor(bit["y1"], bit["x0"])
    item = bit["y0"] + 2 * bit["x0"] + 4 * bit["zl"] + 8 * bit["x1"]
    return item + 16 * first + 32 * second + 64 * third


def columns_of(row, out):
    for part in range(TOKENS // LANES):
        square = jnp.broadcast_to(row[:, part * LANES : (part + 1) * LANES], (LANES, LANES))
        out[pl.ds(part * LANES, LANES), :] = square.T


def lanes_of(rows, out, count, skip):
    lane = lax.broadcasted_iota(jnp.int32, (GROUPS, LANES), 1)
    bands = count * GROUP // LANES
    share = LANES // count
    for band in range(bands):
        packed = jnp.zeros((GROUPS, LANES), jnp.int32)
        for part in range(share):
            some = rows[pl.ds(band * share + part, GROUPS, stride=GROUP), :]
            some = pltpu.roll(some, (part * count - skip) % LANES, axis=1)
            inside = (lane >= part * count) & (lane < (part + 1) * count)
            packed = jnp.where(inside, some, packed)
        out[pl.ds(band, GROUPS, stride=bands), :] = packed


def count_rows(flags):
    rows = flags.shape[0]
    while rows > 8:
        rows //= 2
        flags = flags[:rows] + flags[rows:]
    total = flags[:1]
    for row in range(1, 8):
        total = total + flags[row : row + 1]
    return total


def write_requests(negatives, pos_row, pos_cols, owned, met_ids, asks, slot_cols, rank_cols):
    lane = lax.broadcasted_iota(jnp.int32, (TOKENS, LANES), 1)
    line = lax.broadcasted_iota(jnp.int32, (TOKENS, LANES), 0)
    ids = pos_cols[...]
    slot = slot_of(jnp.right_shift(ids, 12))
    slot_row = slot_of(jnp.right_shift(pos_row[...], 12))
    ranks = []
    for part in range(TOKENS // LANES):
        near = slot_row[:, part * LANES : (part + 1) * LANES]
        earlier = (slot == near) & (line < lane + part * LANES)
        ranks.append(count_rows(jnp.where(earlier, 1, 0)))
    columns_of(jnp.concatenate(ranks, axis=1), rank_cols)
    rank = rank_cols[...]
    slot_cols[...] = slot * CAPACITY + rank
    named = jnp.where(slot == lane, jnp.bitwise_and(ids, ROWS - 1) + 1, 0)
    wanted = [jnp.zeros((PER_OWNER, LANES), jnp.int32)]
    for place in range(CAPACITY):
        wanted.append(count_rows(jnp.where(rank == place, named, 0)))
    wanted.append(jnp.zeros((LANES - ASKED, LANES), jnp.int32))
    wanted = jnp.concatenate(wanted, axis=0).T - 1
    share = LANES // PER_OWNER
    for part in range(share):
        owned[pl.ds(part, DEVICES // share, stride=share), :] = pltpu.roll(
            negatives[...], (LANES - part * PER_OWNER) % LANES, axis=1
        )

    def order(group, _):
        for item, (seq, loop) in enumerate(partners(group)):
            met_ids[pl.ds(group * GROUP + item, 1), :] = owned[pl.ds(seq * 4 + loop, 1), :]
        return 0

    lax.fori_loop(0, GROUPS, order, 0)
    slots = lax.broadcasted_iota(jnp.int32, (DEVICES, LANES), 1)
    asks[...] = jnp.where(
        slots < PER_OWNER, jnp.bitwise_and(met_ids[...], ROWS - 1), wanted
    )


def step_kernel(
    events_in,
    carried_in,
    stamp_row,
    negatives,
    pos_row,
    in_gain,
    w_in_in,
    attn_gain,
    w_out_in,
    table,
    loss_out,
    grad_out,
    total_out,
    events,
    carried,
    w_in,
    w_out,
    far,
    stamp_cols,
    pos_cols,
    slot_cols,
    rank_cols,
    owned,
    met_ids,
    asks,
    asked,
    asked_scalar,
    neg_ids,
    neg_asked,
    pos_asked,
    lines,
    units,
    stage,
    sent,
    answered,
    returned,
    gate,
    queries,
    keys,
    values,
    mixed,
    hidden,
    hidden_unit,
    sums,
    targets,
    inverse,
    d_pos,
    d_state,
    loss,
    grad,
    total,
    load_sems,
    local_sem,
    ask_send,
    ask_recv,
    halo_send,
    halo_recv,
    row_send,
    row_recv,
    back_send,
    back_recv,
    out_sems,
):
    seq, loop = lax.axis_index("seq"), lax.axis_index("loop")
    barrier = pltpu.get_barrier_semaphore()
    each_partner(
        lambda slot, device: pl.semaphore_signal(
            barrier, inc=1, device_id=device, device_id_type=pl.DeviceIdType.MESH
        )
    )
    loads = [
        pltpu.make_async_copy(source, target, load_sems.at[at])
        for at, (source, target) in enumerate(
            [
                (events_in, events),
                (table, units),
                (w_in_in, w_in),
                (w_out_in, w_out),
                (carried_in, carried),
            ]
        )
    ]
    for load in loads:
        load.start()

    def to_partner(source, target, send, recv, device):
        return pltpu.make_async_remote_copy(
            src_ref=source,
            dst_ref=target,
            send_sem=send,
            recv_sem=recv,
            device_id=device,
            device_id_type=pl.DeviceIdType.MESH,
        )

    other = (seq, loop + 1 - 2 * lax.rem(loop, 2))

    def expect(buffer, send, recv):
        return to_partner(buffer, buffer, send, recv, other)

    columns_of(pos_row, pos_cols)
    columns_of(stamp_row, stamp_cols)
    write_requests(
        negatives, pos_row, pos_cols, owned, met_ids, asks, slot_cols, rank_cols
    )
    asked[pl.ds(0, 1), :] = asks[pl.ds(0, 1), :]
    loads[0].wait()
    pl.semaphore_wait(barrier, DEVICES - 1)

    each_partner(
        lambda slot, device: to_partner(
            asks.at[pl.ds(slot, 1)], asked.at[pl.ds(slot, 1)], ask_send, ask_recv, device
        ).start()
    )
    halos = [
        to_partner(
            events,
            far.at[reach - 1],
            halo_send.at[reach - 1],
            halo_recv.at[reach - 1],
            (lax.rem(seq + reach, 32), loop),
        )
        for reach in range(1, WINDOW)
    ]
    for halo in halos:
        halo.start()

    lanes_of(met_ids, neg_ids, PER_OWNER, 0)
    loads[1].wait()
    widen_table(units, lines)
    loads[2].wait()
    project_own(events, in_gain, w_in, gate, queries, keys, values)
    sums[...] = jnp.zeros_like(sums)
    targets[...] = jnp.zeros_like(targets)
    d_state[...] = jnp.zeros_like(d_state)

    others = expect(asked.at[pl.ds(1, DEVICES - 1)], ask_send, ask_recv)
    others.wait_recv()
    scalars = pltpu.make_async_copy(asked, asked_scalar, local_sem)
    scalars.start()
    lanes_of(asked, neg_asked, PER_OWNER, 0)
    lanes_of(asked, pos_asked, CAPACITY, PER_OWNER)
    scalars.wait()

    def send_group(group, target, send, recv):
        for item, device in enumerate(partners(group)):
            slot = group * GROUP + item

            def start(slot=slot, device=device):
                to_partner(sent.at[slot], target.at[slot], send, recv.at[group], device).start()

            if item == 0:
                pl.when(group > 0)(start)
            else:
                start()

        @pl.when(group == 0)
        def _():
            mine = pltpu.make_async_copy(sent.at[0], target.at[0], local_sem)
            mine.start()
            mine.wait()

    def await_group(group, target, send, recv):
        @pl.when(group == 0)
        def _():
            expect(target.at[pl.ds(1, GROUP - 1)], send, recv.at[0]).wait_recv()

        @pl.when(group > 0)
        def _():
            expect(target.at[pl.ds(0, GROUP)], send, recv.at[group]).wait_recv()

    def answer_group(group, _):
        def one(item, _):
            answer(asked_scalar, lines, stage, sent, group * GROUP + item)
            return 0

        lax.fori_loop(0, GROUP, one, 0)
        send_group(group, answered, row_send, row_recv)
        return 0

    lax.fori_loop(0, GROUPS, answer_group, 0)

    def far_block(reach, _):
        expect(far.at[reach - 1], halo_send.at[reach - 1], halo_recv.at[reach - 1]).wait_recv()
        live = jnp.where(seq >= reach, 1.0, 0.0).astype(F32)
        project_far(reach, far[reach - 1], live, in_gain, w_in, keys, values)
        return 0

    lax.fori_loop(1, WINDOW, far_block, 0)
    attend(stamp_cols, stamp_row, queries, keys, values, mixed)
    loads[3].wait()
    loads[4].wait()
    finish_hidden(events, carried, attn_gain, w_out, gate, mixed, hidden)
    unit_hidden(hidden, hidden_unit)

    def meet(group, _):
        await_group(group, answered, row_send, row_recv)
        meet_group(
            group, answered, neg_ids, pos_cols, slot_cols, hidden_unit, units, lines, sums, targets
        )
        return 0

    lax.fori_loop(0, GROUPS, meet, 0)
    d_pos[...] = settle(hidden_unit, sums, targets, loss, inverse)
    expect(sent.at[pl.ds(0, DEVICES - 1)], row_send, row_recv.at[0]).wait_send()

    def back(group, _):
        return_group(
            group, answered, slot_cols, hidden_unit, units, lines, inverse, d_pos, d_state, sent
        )
        send_group(group, returned, back_send, back_recv)
        return 0

    lax.fori_loop(0, GROUPS, back, 0)
    hidden_back(hidden, d_state, targets, grad)
    outs = [
        pltpu.make_async_copy(loss, loss_out, out_sems.at[0]),
        pltpu.make_async_copy(grad, grad_out, out_sems.at[1]),
    ]
    for out in outs:
        out.start()
    total[...] = jnp.zeros_like(total)

    def collect(group, _):
        await_group(group, returned, back_send, back_recv)
        add_group(group, returned, neg_asked, pos_asked, total, lambda start, step: None)
        return 0

    lax.fori_loop(0, GROUPS, collect, 0)
    outs.append(pltpu.make_async_copy(total, total_out, out_sems.at[2]))
    outs[2].start()
    others.wait_send()
    for halo in halos:
        halo.wait_send()
    expect(sent.at[pl.ds(0, DEVICES - 1)], back_send, back_recv.at[0]).wait_send()
    for out in outs:
        out.wait()


def whole(kind, shape):
    return pltpu.VMEM(shape, kind)


def on_device(events, carried, positions, neg_ids, pos_ids, in_gain, w_in, attn_gain, w_out, table):
    inside = pl.BlockSpec(memory_space=pltpu.VMEM)
    outside = pl.BlockSpec(memory_space=pl.ANY)
    integers = jnp.int32
    loss, grad_hidden, grad_table = pl.pallas_call(
        step_kernel,
        out_shape=(
            jax.ShapeDtypeStruct((TOKENS // LANES, LANES), F32),
            jax.ShapeDtypeStruct((TOKENS, WIDTH), BF16),
            jax.ShapeDtypeStruct((ROWS, WIDTH), F32),
        ),
        in_specs=[
            outside,
            outside,
            inside,
            inside,
            inside,
            inside,
            outside,
            inside,
            outside,
            outside,
        ],
        out_specs=(outside, outside, outside),
        scratch_shapes=[
            whole(BF16, (TOKENS, WIDTH)),
            whole(F32, (TOKENS, WIDTH)),
            whole(BF16, (WIDTH, 4 * WIDTH)),
            whole(BF16, (WIDTH, WIDTH)),
            whole(BF16, (WINDOW - 1, TOKENS, WIDTH)),
            whole(integers, (TOKENS, LANES)),
            whole(integers, (TOKENS, LANES)),
            whole(integers, (TOKENS, LANES)),
            whole(integers, (TOKENS, LANES)),
            whole(integers, (DEVICES, LANES)),
            whole(integers, (DEVICES, LANES)),
            whole(integers, (DEVICES, LANES)),
            whole(integers, (DEVICES, LANES)),
            pltpu.SMEM((DEVICES, LANES), integers),
            whole(integers, (GROUPS * BANDS, LANES)),
            whole(integers, (GROUPS * BANDS, LANES)),
            whole(integers, (GROUPS, LANES)),
            whole(F32, (ROWS * BANDS, LANES)),
            whole(BF16, (ROWS, WIDTH)),
            whole(F32, (MESSAGE, LANES)),
            whole(BF16, (DEVICES, MESSAGE, LANES)),
            whole(BF16, (DEVICES, MESSAGE, LANES)),
            whole(BF16, (DEVICES, MESSAGE, LANES)),
            whole(BF16, (TOKENS, WIDTH)),
            whole(BF16, (BANDS, TOKENS, LANES)),
            whole(BF16, (WINDOW, BANDS, TOKENS, LANES)),
            whole(BF16, (WINDOW, BANDS, TOKENS, LANES)),
            whole(F32, (BANDS, TOKENS, LANES)),
            whole(BF16, (TOKENS, WIDTH)),
            whole(BF16, (TOKENS, WIDTH)),
            whole(F32, (TOKENS, LANES)),
            whole(F32, (TOKENS, WIDTH)),
            whole(F32, (TOKENS, LANES)),
            whole(BF16, (TOKENS, WIDTH)),
            whole(F32, (TOKENS, WIDTH)),
            whole(F32, (TOKENS // LANES, LANES)),
            whole(BF16, (TOKENS, WIDTH)),
            whole(F32, (ROWS, WIDTH)),
            pltpu.SemaphoreType.DMA((5,)),
            pltpu.SemaphoreType.DMA,
            pltpu.SemaphoreType.DMA,
            pltpu.SemaphoreType.DMA,
            pltpu.SemaphoreType.DMA((WINDOW - 1,)),
            pltpu.SemaphoreType.DMA((WINDOW - 1,)),
            pltpu.SemaphoreType.DMA,
            pltpu.SemaphoreType.DMA((GROUPS,)),
            pltpu.SemaphoreType.DMA,
            pltpu.SemaphoreType.DMA((GROUPS,)),
            pltpu.SemaphoreType.DMA((3,)),
        ],
        compiler_params=pltpu.CompilerParams(
            collective_id=0, has_side_effects=True, vmem_limit_bytes=BANK
        ),
        name="step",
    )(
        events[0],
        carried[0],
        positions,
        neg_ids.reshape(NEG // LANES, LANES),
        pos_ids,
        in_gain[None, :],
        w_in,
        attn_gain[None, :],
        w_out,
        table,
    )
    return (loss.reshape(1, TOKENS), grad_hidden[None], grad_table)


def solution(mesh):
    return jax.shard_map(
        on_device,
        mesh=mesh,
        in_specs=(
            P("loop", "seq", None),
            P("loop", "seq", None),
            P("loop", "seq"),
            P("loop", "seq", None),
            P("loop", "seq"),
            P(),
            P(),
            P(),
            P(),
            P(("seq", "loop"), None),
        ),
        out_specs=(P("loop", "seq"), P("loop", "seq", None), P(("seq", "loop"), None)),
        check_vma=False,
    )
```

profile of v0, /device:TPU:22, one launch (start us, length us, event | category | flops | bytes accessed | tf_op | source)
XLA Modules:
  0.0 220.6 jit_solution(8692868218835208899)
XLA Ops:
  0.6 209.1 %step.1 = (f32[4,128]{1,0:T(4,128)}, bf16[512,512]{1,0:T(8,128)(2,1)}, f32[4096,512]{1,0:T(8,128)}) custom-call(bf16[512,512]{1,0:T(8,128)(2,1)} %bitcast.8, f32[512,512]{1,0:T(8,128)} %bitcast.7, s32[1,512]{1,0:T(1,128)} %stamp_row.1, s32[32,128]{1,0:T(8,128)} %bitcast.10, s32[1,512]{1,0:T(1,128)} %pos_row.1, f32[1,512]{1,0:T(1,128)} %bitcast.11, ...), custom_call_target="tpu_custom_call" | custom-call | tf_op jit(solution)/shard_map/step/pallas_call | solution.py:689
  209.7 1.2 copy.16
  211.0 1.9 copy.17
  212.8 7.8 %copy.18 = f32[4096,512]{1,0:T(8,128)} copy(f32[4096,512]{1,0:T(8,128)} %get-tuple-element.14) | data formatting | bytes 16777216
where the time goes:
time: 221 us
  Pallas kernels  209 us (95%)
  local copies, waits for them, and re-layouts  10.9 us (5%)
    pallas_call x1, Pallas kernels, on_device(): pl.pallas_call(step_kernel, out_shape=(jax.ShapeDtypeStruct((TOKENS // LA...  209 us
    unnamed x3, local copies, waits for them, and re-layouts  10.9 us

commit v1 on v0

--- a/solution.py
+++ b/solution.py
@@ -1,3 +1,5 @@
+import functools
+
 import jax
 import jax.numpy as jnp
 from jax import lax
@@ -32,6 +34,9 @@
 BF16 = jnp.bfloat16
 NT = (((1,), (1,)), ((), ()))
 TN = (((0,), (0,)), ((), ()))
+TILE = 1024
+END_TILE = 512
+CORNER_TURN, BACK_TURN, FORWARD_TURN = 1, 2, 3
 BANK = 62 * 2**20
 
 
@@ -279,28 +284,50 @@
     grad[...] = (scale * (upstream - unit * row_sum(unit * upstream))).astype(BF16)
 
 
-def add_group(group, message, neg_asked, pos_asked, total, done):
-    negs = neg_rows(message, group)
-    poss = pos_rows(message, group).astype(BF16)
-    step = 512
+def pair_rows(message, group):
+    parts = [neg_rows(message, group), neg_rows(message, group + 1)]
+    parts += [pos_rows(message, at).astype(BF16) for at in (group, group + 1)]
+    return jnp.concatenate(parts, axis=0)
+
+
+def add_tile(start, count, neg_asked, pos_asked, group, rows):
+    row = lax.broadcasted_iota(jnp.int32, (count, LANES), 0) + start
+
+    def hits(asked, line):
+        return jnp.where(row == asked[pl.ds(line, 1), :], 1.0, 0.0).astype(BF16)
+
+    wide = [hits(neg_asked, group * BANDS + band) for band in range(2 * BANDS)]
+    wide += [hits(pos_asked, group), hits(pos_asked, group + 1)]
+    return jnp.dot(jnp.concatenate(wide, axis=1), rows, preferred_element_type=F32)
+
+
+def add_pair(group, message, neg_asked, pos_asked, total):
+    rows = pair_rows(message, group)
 
     def tile(index, _):
-        start = pl.multiple_of(index * step, step)
-        row = lax.broadcasted_iota(jnp.int32, (step, LANES), 0) + start
-
-        def hits(asked, line):
-            return jnp.where(row == asked[pl.ds(line, 1), :], 1.0, 0.0).astype(BF16)
-
-        wide = jnp.concatenate(
-            [hits(neg_asked, group * BANDS + band) for band in range(BANDS)], axis=1
-        )
-        part = jnp.dot(wide, negs, preferred_element_type=F32)
-        part += jnp.dot(hits(pos_asked, group), poss, preferred_element_type=F32)
-        total[pl.ds(start, step), :] += part
-        done(start, step)
-        return 0
-
-    lax.fori_loop(0, ROWS // step, tile, 0)
+        start = pl.multiple_of(index * TILE, TILE)
+        total[pl.ds(start, TILE), :] += add_tile(start, TILE, neg_asked, pos_asked, group, rows)
+        return 0
+
+    lax.fori_loop(0, ROWS // TILE, tile, 0)
+
+
+def finish_kernel(before, message, neg_asked, pos_asked, loss_in, grad_in, total, loss, grad):
+    index = pl.program_id(0)
+
+    @pl.when(index == 0)
+    def _():
+        loss[...] = loss_in[...]
+        grad[...] = grad_in[...]
+
+    total[...] = before[...] + add_tile(
+        index * END_TILE,
+        END_TILE,
+        neg_asked,
+        pos_asked,
+        GROUPS - 2,
+        pair_rows(message, 0),
+    )
 
 
 SEQ_BITS = ("x0", "x1", "zl", "y0", "y1")
@@ -343,15 +370,14 @@
 def each_partner(act):
     def one(group, _):
         for item, device in enumerate(partners(group)):
-            slot = group * GROUP + item
             if item == 0:
 
                 @pl.when(group > 0)
                 def _():
-                    act(slot, device)
+                    act(group, item, device)
 
             else:
-                act(slot, device)
+                act(group, item, device)
         return 0
 
     lax.fori_loop(0, GROUPS, one, 0)
@@ -452,6 +478,9 @@
     loss_out,
     grad_out,
     total_out,
+    last,
+    neg_asked_out,
+    pos_asked_out,
     events,
     carried,
     w_in,
@@ -505,7 +534,7 @@
     seq, loop = lax.axis_index("seq"), lax.axis_index("loop")
     barrier = pltpu.get_barrier_semaphore()
     each_partner(
-        lambda slot, device: pl.semaphore_signal(
+        lambda group, item, device: pl.semaphore_signal(
             barrier, inc=1, device_id=device, device_id_type=pl.DeviceIdType.MESH
         )
     )
@@ -549,80 +578,131 @@
     pl.semaphore_wait(barrier, DEVICES - 1)
 
     each_partner(
-        lambda slot, device: to_partner(
-            asks.at[pl.ds(slot, 1)], asked.at[pl.ds(slot, 1)], ask_send, ask_recv, device
+        lambda group, item, device: to_partner(
+            asks.at[pl.ds(group * GROUP + item, 1)],
+            asked.at[pl.ds(group * GROUP + item, 1)],
+            ask_send,
+            ask_recv.at[group],
+            device,
         ).start()
     )
-    halos = [
-        to_partner(
-            events,
-            far.at[reach - 1],
-            halo_send.at[reach - 1],
-            halo_recv.at[reach - 1],
-            (lax.rem(seq + reach, 32), loop),
-        )
-        for reach in range(1, WINDOW)
+    place = lax.rem(seq, 4)
+    quarter = TOKENS // 4
+
+    def shifted(steps):
+        return (lax.rem(seq + 32 + steps, 32), loop)
+
+    def halo(at, source, target, device):
+        return to_partner(source, target, halo_send.at[at], halo_recv.at[at], device)
+
+    def piece(source, part, device):
+        rows = pl.ds(part * quarter, quarter)
+        return halo(1, far.at[source, rows], far.at[1, rows], device)
+
+    near_halos = [
+        (place < 3, halo(0, events, far.at[0], shifted(1))),
+        (place == 3, halo(3, events, far.at[3], shifted(4))),
+        (place < 4, halo(2, events, far.at[2], shifted(3))),
     ]
-    for halo in halos:
-        halo.start()
+    corner = [(place == 3, halo(0, far.at[3], far.at[0], shifted(-3)))]
+    forward = [
+        (place < 4, piece(0, 0, shifted(1))),
+        (place < 3, piece(0, 1, shifted(1))),
+        (place == 2, piece(0, 2, shifted(1))),
+    ]
+    backward = [
+        (place == 1, piece(2, 1, shifted(-1))),
+        (place > 0, piece(2, 2, shifted(-1))),
+        (place < 4, piece(2, 3, shifted(-1))),
+    ]
+
+    def start_all(copies):
+        for when, copy in copies:
+            pl.when(when)(copy.start)
+
+    def await_halo(at):
+        halo(at, far.at[at], far.at[at], other).wait_recv()
+
+    start_all(near_halos)
 
     lanes_of(met_ids, neg_ids, PER_OWNER, 0)
     loads[1].wait()
     widen_table(units, lines)
+    def send_group(group, target, base, send, recv):
+        for item, device in enumerate(partners(group)):
+
+            def start(item=item, device=device):
+                to_partner(
+                    sent.at[group * GROUP + item],
+                    target.at[(group - base) * GROUP + item],
+                    send,
+                    recv.at[group],
+                    device,
+                ).start()
+
+            if item == 0:
+                pl.when(group > 0)(start)
+            else:
+                start()
+
+    def keep_own(target):
+        mine = pltpu.make_async_copy(sent.at[0], target.at[0], local_sem)
+        mine.start()
+        mine.wait()
+
+    def await_group(group, target, send, recv):
+        @pl.when(group == 0)
+        def _():
+            expect(target.at[pl.ds(1, GROUP - 1)], send, recv.at[0]).wait_recv()
+
+        @pl.when(group > 0)
+        def _():
+            expect(target.at[pl.ds(0, GROUP)], send, recv.at[group]).wait_recv()
+
+    def answer_group(group, _):
+        start = pl.multiple_of(group * GROUP, GROUP)
+        await_group(group, asked, ask_send, ask_recv)
+        scalars = pltpu.make_async_copy(
+            asked.at[pl.ds(start, GROUP)], asked_scalar.at[pl.ds(start, GROUP)], local_sem
+        )
+        scalars.start()
+        scalars.wait()
+
+        def one(item, _):
+            answer(asked_scalar, lines, stage, sent, group * GROUP + item)
+            return 0
+
+        lax.fori_loop(0, GROUP, one, 0)
+        send_group(group, answered, 0, row_send, row_recv)
+        @pl.when(group == CORNER_TURN)
+        def _():
+            pl.when(place == 3)(functools.partial(await_halo, 3))
+            start_all(corner)
+
+        @pl.when(group == BACK_TURN)
+        def _():
+            await_halo(2)
+            start_all(backward)
+
+        @pl.when(group == FORWARD_TURN)
+        def _():
+            await_halo(0)
+            start_all(forward)
+
+        return 0
+
+    lax.fori_loop(0, GROUPS, answer_group, 0)
+    keep_own(answered)
     loads[2].wait()
     project_own(events, in_gain, w_in, gate, queries, keys, values)
     sums[...] = jnp.zeros_like(sums)
     targets[...] = jnp.zeros_like(targets)
     d_state[...] = jnp.zeros_like(d_state)
-
-    others = expect(asked.at[pl.ds(1, DEVICES - 1)], ask_send, ask_recv)
-    others.wait_recv()
-    scalars = pltpu.make_async_copy(asked, asked_scalar, local_sem)
-    scalars.start()
     lanes_of(asked, neg_asked, PER_OWNER, 0)
     lanes_of(asked, pos_asked, CAPACITY, PER_OWNER)
-    scalars.wait()
-
-    def send_group(group, target, send, recv):
-        for item, device in enumerate(partners(group)):
-            slot = group * GROUP + item
-
-            def start(slot=slot, device=device):
-                to_partner(sent.at[slot], target.at[slot], send, recv.at[group], device).start()
-
-            if item == 0:
-                pl.when(group > 0)(start)
-            else:
-                start()
-
-        @pl.when(group == 0)
-        def _():
-            mine = pltpu.make_async_copy(sent.at[0], target.at[0], local_sem)
-            mine.start()
-            mine.wait()
-
-    def await_group(group, target, send, recv):
-        @pl.when(group == 0)
-        def _():
-            expect(target.at[pl.ds(1, GROUP - 1)], send, recv.at[0]).wait_recv()
-
-        @pl.when(group > 0)
-        def _():
-            expect(target.at[pl.ds(0, GROUP)], send, recv.at[group]).wait_recv()
-
-    def answer_group(group, _):
-        def one(item, _):
-            answer(asked_scalar, lines, stage, sent, group * GROUP + item)
-            return 0
-
-        lax.fori_loop(0, GROUP, one, 0)
-        send_group(group, answered, row_send, row_recv)
-        return 0
-
-    lax.fori_loop(0, GROUPS, answer_group, 0)
+    await_halo(1)
 
     def far_block(reach, _):
-        expect(far.at[reach - 1], halo_send.at[reach - 1], halo_recv.at[reach - 1]).wait_recv()
         live = jnp.where(seq >= reach, 1.0, 0.0).astype(F32)
         project_far(reach, far[reach - 1], live, in_gain, w_in, keys, values)
         return 0
@@ -649,33 +729,54 @@
         return_group(
             group, answered, slot_cols, hidden_unit, units, lines, inverse, d_pos, d_state, sent
         )
-        send_group(group, returned, back_send, back_recv)
-        return 0
-
-    lax.fori_loop(0, GROUPS, back, 0)
+        send_group(group, returned, 0, back_send, back_recv)
+        return 0
+
+    lax.fori_loop(0, GROUPS - 2, back, 0)
+
+    def back_last(group, _):
+        return_group(
+            group, answered, slot_cols, hidden_unit, units, lines, inverse, d_pos, d_state, sent
+        )
+        send_group(group, last, GROUPS - 2, back_send, back_recv)
+        return 0
+
+    lax.fori_loop(GROUPS - 2, GROUPS, back_last, 0)
+    keep_own(returned)
     hidden_back(hidden, d_state, targets, grad)
+    total[...] = jnp.zeros_like(total)
+
+    def collect(pair, _):
+        await_group(2 * pair, returned, back_send, back_recv)
+        await_group(2 * pair + 1, returned, back_send, back_recv)
+        add_pair(2 * pair, returned, neg_asked, pos_asked, total)
+        return 0
+
+    lax.fori_loop(0, GROUPS // 2 - 1, collect, 0)
     outs = [
-        pltpu.make_async_copy(loss, loss_out, out_sems.at[0]),
-        pltpu.make_async_copy(grad, grad_out, out_sems.at[1]),
+        pltpu.make_async_copy(source, target, out_sems.at[at])
+        for at, (source, target) in enumerate(
+            [
+                (total, total_out),
+                (loss, loss_out),
+                (grad, grad_out),
+                (neg_asked, neg_asked_out),
+                (pos_asked, pos_asked_out),
+            ]
+        )
     ]
     for out in outs:
         out.start()
-    total[...] = jnp.zeros_like(total)
-
-    def collect(group, _):
-        await_group(group, returned, back_send, back_recv)
-        add_group(group, returned, neg_asked, pos_asked, total, lambda start, step: None)
-        return 0
-
-    lax.fori_loop(0, GROUPS, collect, 0)
-    outs.append(pltpu.make_async_copy(total, total_out, out_sems.at[2]))
-    outs[2].start()
-    others.wait_send()
-    for halo in halos:
-        halo.wait_send()
+    expect(asked.at[pl.ds(1, DEVICES - 1)], ask_send, ask_recv.at[0]).wait_send()
+    for when, copy in near_halos + corner + forward + backward:
+        pl.when(when)(copy.wait_send)
     expect(sent.at[pl.ds(0, DEVICES - 1)], back_send, back_recv.at[0]).wait_send()
     for out in outs:
         out.wait()
+    for end in range(2):
+        expect(
+            last.at[pl.ds(end * GROUP, GROUP)], back_send, back_recv.at[GROUPS - 2 + end]
+        ).wait_recv()
 
 
 def whole(kind, shape):
@@ -686,12 +787,15 @@
     inside = pl.BlockSpec(memory_space=pltpu.VMEM)
     outside = pl.BlockSpec(memory_space=pl.ANY)
     integers = jnp.int32
-    loss, grad_hidden, grad_table = pl.pallas_call(
+    loss, grad_hidden, most, last, neg_asked, pos_asked = pl.pallas_call(
         step_kernel,
         out_shape=(
             jax.ShapeDtypeStruct((TOKENS // LANES, LANES), F32),
             jax.ShapeDtypeStruct((TOKENS, WIDTH), BF16),
             jax.ShapeDtypeStruct((ROWS, WIDTH), F32),
+            jax.ShapeDtypeStruct((2 * GROUP, MESSAGE, LANES), BF16),
+            jax.ShapeDtypeStruct((GROUPS * BANDS, LANES), integers),
+            jax.ShapeDtypeStruct((GROUPS, LANES), integers),
         ),
         in_specs=[
             outside,
@@ -705,13 +809,13 @@
             outside,
             outside,
         ],
-        out_specs=(outside, outside, outside),
+        out_specs=(outside,) * 6,
         scratch_shapes=[
             whole(BF16, (TOKENS, WIDTH)),
             whole(F32, (TOKENS, WIDTH)),
             whole(BF16, (WIDTH, 4 * WIDTH)),
             whole(BF16, (WIDTH, WIDTH)),
-            whole(BF16, (WINDOW - 1, TOKENS, WIDTH)),
+            whole(BF16, (WINDOW, TOKENS, WIDTH)),
             whole(integers, (TOKENS, LANES)),
             whole(integers, (TOKENS, LANES)),
             whole(integers, (TOKENS, LANES)),
@@ -729,7 +833,7 @@
             whole(F32, (MESSAGE, LANES)),
             whole(BF16, (DEVICES, MESSAGE, LANES)),
             whole(BF16, (DEVICES, MESSAGE, LANES)),
-            whole(BF16, (DEVICES, MESSAGE, LANES)),
+            whole(BF16, (DEVICES - 2 * GROUP, MESSAGE, LANES)),
             whole(BF16, (TOKENS, WIDTH)),
             whole(BF16, (BANDS, TOKENS, LANES)),
             whole(BF16, (WINDOW, BANDS, TOKENS, LANES)),
@@ -748,14 +852,14 @@
             pltpu.SemaphoreType.DMA((5,)),
             pltpu.SemaphoreType.DMA,
             pltpu.SemaphoreType.DMA,
-            pltpu.SemaphoreType.DMA,
-            pltpu.SemaphoreType.DMA((WINDOW - 1,)),
-            pltpu.SemaphoreType.DMA((WINDOW - 1,)),
+            pltpu.SemaphoreType.DMA((GROUPS,)),
+            pltpu.SemaphoreType.DMA((4,)),
+            pltpu.SemaphoreType.DMA((4,)),
             pltpu.SemaphoreType.DMA,
             pltpu.SemaphoreType.DMA((GROUPS,)),
             pltpu.SemaphoreType.DMA,
             pltpu.SemaphoreType.DMA((GROUPS,)),
-            pltpu.SemaphoreType.DMA((3,)),
+            pltpu.SemaphoreType.DMA((5,)),
         ],
         compiler_params=pltpu.CompilerParams(
             collective_id=0, has_side_effects=True, vmem_limit_bytes=BANK
@@ -773,6 +877,24 @@
         w_out,
         table,
     )
+    fixed = [most, last, neg_asked, pos_asked, loss, grad_hidden]
+    tile = pl.BlockSpec((END_TILE, WIDTH), lambda index: (index, 0))
+    rest = [
+        pl.BlockSpec(array.shape, lambda index, rank=array.ndim: (0,) * rank) for array in fixed[1:]
+    ]
+    grad_table, loss, grad_hidden = pl.pallas_call(
+        finish_kernel,
+        grid=(ROWS // END_TILE,),
+        out_shape=(
+            jax.ShapeDtypeStruct((ROWS, WIDTH), F32),
+            jax.ShapeDtypeStruct(loss.shape, F32),
+            jax.ShapeDtypeStruct(grad_hidden.shape, BF16),
+        ),
+        in_specs=[tile] + rest,
+        out_specs=(tile, rest[3], rest[4]),
+        compiler_params=pltpu.CompilerParams(vmem_limit_bytes=BANK),
+        name="finish",
+    )(*fixed)
     return (loss.reshape(1, TOKENS), grad_hidden[None], grad_table)
 
 

time: 221 us -> 202 us (0.914)
  the two profiles are of different devices: /device:TPU:22 before, /device:TPU:16 now
where the time goes in v1:
time: 202 us; the launch traced here: 200 us
  Pallas kernels  199 us (99%)
    pallas_call x1, Pallas kernels, on_device(): pl.pallas_call(step_kernel, out_shape=(jax.ShapeDtypeStruct((TOKENS // LA...  187 us
    pallas_call x1, Pallas kernels, on_device(): pl.pallas_call(finish_kernel, grid=(ROWS // END_TILE,), out_shape=(jax.Sh...  12.2 us

profile of v1, /device:TPU:16, one launch (start us, length us, event | category | flops | bytes accessed | tf_op | source)
XLA Modules:
  0.0 199.7 jit_solution(4698565410023929678)
XLA Ops:
  0.6 186.9 %step.1 = (f32[4,128]{1,0:T(4,128)}, bf16[512,512]{1,0:T(8,128)(2,1)}, f32[4096,512]{1,0:T(8,128)}, bf16[32,160,128]{2,1,0:T(8,128)(2,1)}, s32[32,128]{1,0:T(8,128)}, /*index=5*/s32[8,128]{1,0:T(8,128)}) custom-call(bf16[512,512]{1,0:T(8,128)(2,1)} %bitcast.8, f32[512,512]{1,0:T(8,128)} %bitcast.7, s32[1,512]{1,0:T(1,128)} %stamp_row.1, s32[32,128]{1,0:T(8,128)} %bitcast.9, ...), custom_call_target="tpu_custom_call" | custom-call | tf_op jit(solution)/shard_map/step/pallas_call | solution.py:790
  187.5 12.2 %finish.1 = (f32[4096,512]{1,0:T(8,128)}, f32[4,128]{1,0:T(4,128)}, bf16[512,512]{1,0:T(8,128)(2,1)}) custom-call(f32[4096,512]{1,0:T(8,128)} %get-tuple-element.12.before, bf16[32,160,128]{2,1,0:T(8,128)(2,1)} %get-tuple-element.13.message, s32[32,128]{1,0:T(8,128)} %get-tuple-element.14.neg_asked, s32[8,128]{1,0:T(8,128)} %get-tuple-element.15.pos_asked, ...), custom_call_target="tpu_custom_call" | custom-call | tf_op jit(solution)/shard_map/finish/pallas_call | solution.py:885

commit v2 on v1

--- a/solution.py
+++ b/solution.py
@@ -36,7 +36,7 @@
 TN = (((0,), (0,)), ((), ()))
 TILE = 1024
 END_TILE = 512
-CORNER_TURN, BACK_TURN, FORWARD_TURN = 1, 2, 3
+CORNER_TURN, BACK_TURN, FORWARD_TURN = 3, 4, 5
 BANK = 62 * 2**20
 
 
@@ -284,29 +284,31 @@
     grad[...] = (scale * (upstream - unit * row_sum(unit * upstream))).astype(BF16)
 
 
-def pair_rows(message, group):
-    parts = [neg_rows(message, group), neg_rows(message, group + 1)]
-    parts += [pos_rows(message, at).astype(BF16) for at in (group, group + 1)]
+def group_rows(message, groups):
+    parts = [neg_rows(message, group) for group in groups]
+    parts += [pos_rows(message, group).astype(BF16) for group in groups]
     return jnp.concatenate(parts, axis=0)
 
 
-def add_tile(start, count, neg_asked, pos_asked, group, rows):
+def add_tile(start, count, neg_asked, pos_asked, groups, rows):
     row = lax.broadcasted_iota(jnp.int32, (count, LANES), 0) + start
 
     def hits(asked, line):
         return jnp.where(row == asked[pl.ds(line, 1), :], 1.0, 0.0).astype(BF16)
 
-    wide = [hits(neg_asked, group * BANDS + band) for band in range(2 * BANDS)]
-    wide += [hits(pos_asked, group), hits(pos_asked, group + 1)]
+    wide = [
+        hits(neg_asked, group * BANDS + band) for group in groups for band in range(BANDS)
+    ]
+    wide += [hits(pos_asked, group) for group in groups]
     return jnp.dot(jnp.concatenate(wide, axis=1), rows, preferred_element_type=F32)
 
 
-def add_pair(group, message, neg_asked, pos_asked, total):
-    rows = pair_rows(message, group)
+def add_groups(groups, message, neg_asked, pos_asked, total):
+    rows = group_rows(message, groups)
 
     def tile(index, _):
         start = pl.multiple_of(index * TILE, TILE)
-        total[pl.ds(start, TILE), :] += add_tile(start, TILE, neg_asked, pos_asked, group, rows)
+        total[pl.ds(start, TILE), :] += add_tile(start, TILE, neg_asked, pos_asked, groups, rows)
         return 0
 
     lax.fori_loop(0, ROWS // TILE, tile, 0)
@@ -320,13 +322,14 @@
         loss[...] = loss_in[...]
         grad[...] = grad_in[...]
 
-    total[...] = before[...] + add_tile(
-        index * END_TILE,
+    start = pl.multiple_of(index * END_TILE, END_TILE)
+    total[...] = before[pl.ds(start, END_TILE), :] + add_tile(
+        start,
         END_TILE,
         neg_asked,
         pos_asked,
-        GROUPS - 2,
-        pair_rows(message, 0),
+        [GROUPS - 1],
+        group_rows(message, [0]),
     )
 
 
@@ -475,12 +478,12 @@
     attn_gain,
     w_out_in,
     table,
-    loss_out,
-    grad_out,
-    total_out,
+    loss,
+    grad,
+    total,
     last,
-    neg_asked_out,
-    pos_asked_out,
+    neg_asked,
+    pos_asked,
     events,
     carried,
     w_in,
@@ -496,8 +499,6 @@
     asked,
     asked_scalar,
     neg_ids,
-    neg_asked,
-    pos_asked,
     lines,
     units,
     stage,
@@ -516,9 +517,6 @@
     inverse,
     d_pos,
     d_state,
-    loss,
-    grad,
-    total,
     load_sems,
     local_sem,
     ask_send,
@@ -529,7 +527,6 @@
     row_recv,
     back_send,
     back_recv,
-    out_sems,
 ):
     seq, loop = lax.axis_index("seq"), lax.axis_index("loop")
     barrier = pltpu.get_barrier_semaphore()
@@ -732,16 +729,16 @@
         send_group(group, returned, 0, back_send, back_recv)
         return 0
 
-    lax.fori_loop(0, GROUPS - 2, back, 0)
+    lax.fori_loop(0, GROUPS - 1, back, 0)
 
     def back_last(group, _):
         return_group(
             group, answered, slot_cols, hidden_unit, units, lines, inverse, d_pos, d_state, sent
         )
-        send_group(group, last, GROUPS - 2, back_send, back_recv)
-        return 0
-
-    lax.fori_loop(GROUPS - 2, GROUPS, back_last, 0)
+        send_group(group, last, GROUPS - 1, back_send, back_recv)
+        return 0
+
+    lax.fori_loop(GROUPS - 1, GROUPS, back_last, 0)
     keep_own(returned)
     hidden_back(hidden, d_state, targets, grad)
     total[...] = jnp.zeros_like(total)
@@ -749,34 +746,18 @@
     def collect(pair, _):
         await_group(2 * pair, returned, back_send, back_recv)
         await_group(2 * pair + 1, returned, back_send, back_recv)
-        add_pair(2 * pair, returned, neg_asked, pos_asked, total)
+        add_groups([2 * pair, 2 * pair + 1], returned, neg_asked, pos_asked, total)
         return 0
 
     lax.fori_loop(0, GROUPS // 2 - 1, collect, 0)
-    outs = [
-        pltpu.make_async_copy(source, target, out_sems.at[at])
-        for at, (source, target) in enumerate(
-            [
-                (total, total_out),
-                (loss, loss_out),
-                (grad, grad_out),
-                (neg_asked, neg_asked_out),
-                (pos_asked, pos_asked_out),
-            ]
-        )
-    ]
-    for out in outs:
-        out.start()
+    left = jnp.int32(GROUPS - 2)
+    await_group(left, returned, back_send, back_recv)
+    add_groups([left], returned, neg_asked, pos_asked, total)
     expect(asked.at[pl.ds(1, DEVICES - 1)], ask_send, ask_recv.at[0]).wait_send()
     for when, copy in near_halos + corner + forward + backward:
         pl.when(when)(copy.wait_send)
     expect(sent.at[pl.ds(0, DEVICES - 1)], back_send, back_recv.at[0]).wait_send()
-    for out in outs:
-        out.wait()
-    for end in range(2):
-        expect(
-            last.at[pl.ds(end * GROUP, GROUP)], back_send, back_recv.at[GROUPS - 2 + end]
-        ).wait_recv()
+    expect(last, back_send, back_recv.at[GROUPS - 1]).wait_recv()
 
 
 def whole(kind, shape):
@@ -790,12 +771,12 @@
     loss, grad_hidden, most, last, neg_asked, pos_asked = pl.pallas_call(
         step_kernel,
         out_shape=(
-            jax.ShapeDtypeStruct((TOKENS // LANES, LANES), F32),
-            jax.ShapeDtypeStruct((TOKENS, WIDTH), BF16),
-            jax.ShapeDtypeStruct((ROWS, WIDTH), F32),
-            jax.ShapeDtypeStruct((2 * GROUP, MESSAGE, LANES), BF16),
-            jax.ShapeDtypeStruct((GROUPS * BANDS, LANES), integers),
-            jax.ShapeDtypeStruct((GROUPS, LANES), integers),
+            pltpu.VMEM((TOKENS // LANES, LANES), F32),
+            pltpu.VMEM((TOKENS, WIDTH), BF16),
+            pltpu.VMEM((ROWS, WIDTH), F32),
+            pltpu.VMEM((GROUP, MESSAGE, LANES), BF16),
+            pltpu.VMEM((GROUPS * BANDS, LANES), integers),
+            pltpu.VMEM((GROUPS, LANES), integers),
         ),
         in_specs=[
             outside,
@@ -809,7 +790,7 @@
             outside,
             outside,
         ],
-        out_specs=(outside,) * 6,
+        out_specs=(inside,) * 6,
         scratch_shapes=[
             whole(BF16, (TOKENS, WIDTH)),
             whole(F32, (TOKENS, WIDTH)),
@@ -826,14 +807,12 @@
             whole(integers, (DEVICES, LANES)),
             pltpu.SMEM((DEVICES, LANES), integers),
             whole(integers, (GROUPS * BANDS, LANES)),
-            whole(integers, (GROUPS * BANDS, LANES)),
-            whole(integers, (GROUPS, LANES)),
             whole(F32, (ROWS * BANDS, LANES)),
             whole(BF16, (ROWS, WIDTH)),
             whole(F32, (MESSAGE, LANES)),
             whole(BF16, (DEVICES, MESSAGE, LANES)),
             whole(BF16, (DEVICES, MESSAGE, LANES)),
-            whole(BF16, (DEVICES - 2 * GROUP, MESSAGE, LANES)),
+            whole(BF16, (DEVICES - GROUP, MESSAGE, LANES)),
             whole(BF16, (TOKENS, WIDTH)),
             whole(BF16, (BANDS, TOKENS, LANES)),
             whole(BF16, (WINDOW, BANDS, TOKENS, LANES)),
@@ -846,9 +825,6 @@
             whole(F32, (TOKENS, LANES)),
             whole(BF16, (TOKENS, WIDTH)),
             whole(F32, (TOKENS, WIDTH)),
-            whole(F32, (TOKENS // LANES, LANES)),
-            whole(BF16, (TOKENS, WIDTH)),
-            whole(F32, (ROWS, WIDTH)),
             pltpu.SemaphoreType.DMA((5,)),
             pltpu.SemaphoreType.DMA,
             pltpu.SemaphoreType.DMA,
@@ -859,10 +835,9 @@
             pltpu.SemaphoreType.DMA((GROUPS,)),
             pltpu.SemaphoreType.DMA,
             pltpu.SemaphoreType.DMA((GROUPS,)),
-            pltpu.SemaphoreType.DMA((5,)),
         ],
         compiler_params=pltpu.CompilerParams(
-            collective_id=0, has_side_effects=True, vmem_limit_bytes=BANK
+            collective_id=0, has_side_effects=True, vmem_limit_bytes=52 * 2**20
         ),
         name="step",
     )(
@@ -879,9 +854,7 @@
     )
     fixed = [most, last, neg_asked, pos_asked, loss, grad_hidden]
     tile = pl.BlockSpec((END_TILE, WIDTH), lambda index: (index, 0))
-    rest = [
-        pl.BlockSpec(array.shape, lambda index, rank=array.ndim: (0,) * rank) for array in fixed[1:]
-    ]
+    rest = [pl.BlockSpec(array.shape, lambda index: (0, 0)) for array in (loss, grad_hidden)]
     grad_table, loss, grad_hidden = pl.pallas_call(
         finish_kernel,
         grid=(ROWS // END_TILE,),
@@ -890,9 +863,9 @@
             jax.ShapeDtypeStruct(loss.shape, F32),
             jax.ShapeDtypeStruct(grad_hidden.shape, BF16),
         ),
-        in_specs=[tile] + rest,
-        out_specs=(tile, rest[3], rest[4]),
-        compiler_params=pltpu.CompilerParams(vmem_limit_bytes=BANK),
+        in_specs=[inside] * 6,
+        out_specs=[tile] + rest,
+        compiler_params=pltpu.CompilerParams(vmem_limit_bytes=24 * 2**20),
         name="finish",
     )(*fixed)
     return (loss.reshape(1, TOKENS), grad_hidden[None], grad_table)

time: 202 us -> 189 us (0.936)
  Pallas kernels: 199 us -> 188 us
    pallas_call x1, Pallas kernels: 187 us -> 181 us  [on_device(): pl.pallas_call(step_kernel, out_shape=(pltpu.VMEM((TOKENS // LANES, LANES...]
    pallas_call x1, Pallas kernels: 12.2 us -> 6.84 us  [on_device(): pl.pallas_call(finish_kernel, grid=(ROWS // END_TILE,), out_shape=(jax.Sh...]
where the time goes in v2:
time: 189 us; the launch traced here: 188 us
  Pallas kernels  188 us (99%)
    pallas_call x1, Pallas kernels, on_device(): pl.pallas_call(step_kernel, out_shape=(pltpu.VMEM((TOKENS // LANES, LANES...  181 us
    pallas_call x1, Pallas kernels, on_device(): pl.pallas_call(finish_kernel, grid=(ROWS // END_TILE,), out_shape=(jax.Sh...  6.84 us

profile of v2, /device:TPU:16, one launch (start us, length us, event | category | flops | bytes accessed | tf_op | source)
XLA Modules:
  0.0 188.5 jit_solution(12849613950062612887)
XLA Ops:
  0.6 181.0 %step.1 = (f32[4,128]{1,0:T(4,128)S(1)}, bf16[512,512]{1,0:T(8,128)(2,1)S(1)}, f32[4096,512]{1,0:T(8,128)S(1)}, bf16[16,160,128]{2,1,0:T(8,128)(2,1)S(1)}, s32[32,128]{1,0:T(8,128)S(1)}, /*index=5*/s32[8,128]{1,0:T(8,128)S(1)}) custom-call(bf16[512,512]{1,0:T(8,128)(2,1)} %bitcast.8, f32[512,512]{1,0:T(8,128)} %bitcast.7, s32[1,512]{1,0:T(1,128)} %stamp_row.1, ...), custom_call_target="tpu_custom_call" | custom-call | tf_op jit(solution)/shard_map/step/pallas_call | solution.py:771
  181.7 6.8 %finish.1 = (f32[4096,512]{1,0:T(8,128)}, f32[4,128]{1,0:T(4,128)}, bf16[512,512]{1,0:T(8,128)(2,1)}) custom-call(f32[4096,512]{1,0:T(8,128)S(1)} %get-tuple-element.12.before, bf16[16,160,128]{2,1,0:T(8,128)(2,1)S(1)} %get-tuple-element.13.message, s32[32,128]{1,0:T(8,128)S(1)} %get-tuple-element.14.neg_asked, s32[8,128]{1,0:T(8,128)S(1)} %get-tuple-element.15.pos_asked, ...), custom_call_target="tpu_custom_call" | custom-call | tf_op jit(solution)/shard_map/finish/pallas_call | solution.py:858

commit v3 on v2

--- a/solution.py
+++ b/solution.py
@@ -36,7 +36,10 @@
 TN = (((0,), (0,)), ((), ()))
 TILE = 1024
 END_TILE = 512
-CORNER_TURN, BACK_TURN, FORWARD_TURN = 3, 4, 5
+HELD = 8
+SAME_X = (0, 1, 4, 5)
+OTHER_X = (2, 3, 6, 7, 8, 9, 10, 11, 12, 13, 14, 15)
+CORNER_TURN, BACK_TURN, FORWARD_TURN = 4, 0, 1
 BANK = 62 * 2**20
 
 
@@ -328,8 +331,8 @@
         END_TILE,
         neg_asked,
         pos_asked,
-        [GROUPS - 1],
-        group_rows(message, [0]),
+        [GROUPS - 2, GROUPS - 1],
+        group_rows(message, [0, 1]),
     )
 
 
@@ -603,12 +606,13 @@
     ]
     corner = [(place == 3, halo(0, far.at[3], far.at[0], shifted(-3)))]
     forward = [
-        (place < 4, piece(0, 0, shifted(1))),
-        (place < 3, piece(0, 1, shifted(1))),
+        (place > 0, piece(0, 0, shifted(1))),
+        ((place == 1) | (place == 2), piece(0, 1, shifted(1))),
         (place == 2, piece(0, 2, shifted(1))),
     ]
     backward = [
-        (place == 1, piece(2, 1, shifted(-1))),
+        (place == 2, piece(2, 0, shifted(-1))),
+        ((place == 1) | (place == 2), piece(2, 1, shifted(-1))),
         (place > 0, piece(2, 2, shifted(-1))),
         (place < 4, piece(2, 3, shifted(-1))),
     ]
@@ -625,8 +629,10 @@
     lanes_of(met_ids, neg_ids, PER_OWNER, 0)
     loads[1].wait()
     widen_table(units, lines)
-    def send_group(group, target, base, send, recv):
+    def send_group(group, target, base, send, recv, items=range(GROUP)):
         for item, device in enumerate(partners(group)):
+            if item not in items:
+                continue
 
             def start(item=item, device=device):
                 to_partner(
@@ -670,12 +676,24 @@
             return 0
 
         lax.fori_loop(0, GROUP, one, 0)
-        send_group(group, answered, 0, row_send, row_recv)
         @pl.when(group == CORNER_TURN)
         def _():
             pl.when(place == 3)(functools.partial(await_halo, 3))
             start_all(corner)
 
+        early = group < HELD
+
+        @pl.when(early)
+        def _():
+            send_group(group, answered, 0, row_send, row_recv, SAME_X)
+
+        @pl.when(group >= HELD)
+        def _():
+            send_group(group, answered, 0, row_send, row_recv)
+
+        return 0
+
+    def send_held(group, _):
         @pl.when(group == BACK_TURN)
         def _():
             await_halo(2)
@@ -683,21 +701,26 @@
 
         @pl.when(group == FORWARD_TURN)
         def _():
-            await_halo(0)
+            pl.when(place > 0)(functools.partial(await_halo, 0))
             start_all(forward)
 
-        return 0
-
-    lax.fori_loop(0, GROUPS, answer_group, 0)
+        send_group(group, answered, 0, row_send, row_recv, OTHER_X)
+        return 0
+
+    lax.fori_loop(0, HELD, answer_group, 0)
+    lax.fori_loop(0, HELD, send_held, 0)
+    lax.fori_loop(HELD, GROUPS, answer_group, 0)
     keep_own(answered)
     loads[2].wait()
     project_own(events, in_gain, w_in, gate, queries, keys, values)
     sums[...] = jnp.zeros_like(sums)
     targets[...] = jnp.zeros_like(targets)
     d_state[...] = jnp.zeros_like(d_state)
+    total[...] = jnp.zeros_like(total)
     lanes_of(asked, neg_asked, PER_OWNER, 0)
     lanes_of(asked, pos_asked, CAPACITY, PER_OWNER)
     await_halo(1)
+    pl.when(place == 0)(functools.partial(await_halo, 0))
 
     def far_block(reach, _):
         live = jnp.where(seq >= reach, 1.0, 0.0).astype(F32)
@@ -729,19 +752,18 @@
         send_group(group, returned, 0, back_send, back_recv)
         return 0
 
-    lax.fori_loop(0, GROUPS - 1, back, 0)
+    lax.fori_loop(0, GROUPS - 2, back, 0)
 
     def back_last(group, _):
         return_group(
             group, answered, slot_cols, hidden_unit, units, lines, inverse, d_pos, d_state, sent
         )
-        send_group(group, last, GROUPS - 1, back_send, back_recv)
-        return 0
-
-    lax.fori_loop(GROUPS - 1, GROUPS, back_last, 0)
+        send_group(group, last, GROUPS - 2, back_send, back_recv)
+        return 0
+
+    lax.fori_loop(GROUPS - 2, GROUPS, back_last, 0)
     keep_own(returned)
     hidden_back(hidden, d_state, targets, grad)
-    total[...] = jnp.zeros_like(total)
 
     def collect(pair, _):
         await_group(2 * pair, returned, back_send, back_recv)
@@ -750,14 +772,14 @@
         return 0
 
     lax.fori_loop(0, GROUPS // 2 - 1, collect, 0)
-    left = jnp.int32(GROUPS - 2)
-    await_group(left, returned, back_send, back_recv)
-    add_groups([left], returned, neg_asked, pos_asked, total)
     expect(asked.at[pl.ds(1, DEVICES - 1)], ask_send, ask_recv.at[0]).wait_send()
     for when, copy in near_halos + corner + forward + backward:
         pl.when(when)(copy.wait_send)
     expect(sent.at[pl.ds(0, DEVICES - 1)], back_send, back_recv.at[0]).wait_send()
-    expect(last, back_send, back_recv.at[GROUPS - 1]).wait_recv()
+    for end in range(2):
+        expect(
+            last.at[pl.ds(end * GROUP, GROUP)], back_send, back_recv.at[GROUPS - 2 + end]
+        ).wait_recv()
 
 
 def whole(kind, shape):
@@ -774,7 +796,7 @@
             pltpu.VMEM((TOKENS // LANES, LANES), F32),
             pltpu.VMEM((TOKENS, WIDTH), BF16),
             pltpu.VMEM((ROWS, WIDTH), F32),
-            pltpu.VMEM((GROUP, MESSAGE, LANES), BF16),
+            pltpu.VMEM((2 * GROUP, MESSAGE, LANES), BF16),
             pltpu.VMEM((GROUPS * BANDS, LANES), integers),
             pltpu.VMEM((GROUPS, LANES), integers),
         ),
@@ -812,7 +834,7 @@
             whole(F32, (MESSAGE, LANES)),
             whole(BF16, (DEVICES, MESSAGE, LANES)),
             whole(BF16, (DEVICES, MESSAGE, LANES)),
-            whole(BF16, (DEVICES - GROUP, MESSAGE, LANES)),
+            whole(BF16, (DEVICES - 2 * GROUP, MESSAGE, LANES)),
             whole(BF16, (TOKENS, WIDTH)),
             whole(BF16, (BANDS, TOKENS, LANES)),
             whole(BF16, (WINDOW, BANDS, TOKENS, LANES)),

time: 189 us -> 187 us (0.989)
  the two profiles are of different devices: /device:TPU:16 before, /device:TPU:1 now
where the time goes in v3:
time: 187 us
  Pallas kernels  186 us (99%)
    pallas_call x1, Pallas kernels, on_device(): pl.pallas_call(step_kernel, out_shape=(pltpu.VMEM((TOKENS // LANES, LANES...  178 us
    pallas_call x1, Pallas kernels, on_device(): pl.pallas_call(finish_kernel, grid=(ROWS // END_TILE,), out_shape=(jax.Sh...  8.18 us

profile of v3, /device:TPU:1, one launch (start us, length us, event | category | flops | bytes accessed | tf_op | source)
XLA Modules:
  0.0 187.0 jit_solution(11549837014801657455)
XLA Ops:
  0.6 178.2 %step.1 = (f32[4,128]{1,0:T(4,128)S(1)}, bf16[512,512]{1,0:T(8,128)(2,1)S(1)}, f32[4096,512]{1,0:T(8,128)S(1)}, bf16[32,160,128]{2,1,0:T(8,128)(2,1)S(1)}, s32[32,128]{1,0:T(8,128)S(1)}, /*index=5*/s32[8,128]{1,0:T(8,128)S(1)}) custom-call(bf16[512,512]{1,0:T(8,128)(2,1)} %bitcast.8, f32[512,512]{1,0:T(8,128)} %bitcast.7, s32[1,512]{1,0:T(1,128)} %stamp_row.1, ...), custom_call_target="tpu_custom_call" | custom-call | tf_op jit(solution)/shard_map/step/pallas_call | solution.py:793
  178.8 8.2 %finish.1 = (f32[4096,512]{1,0:T(8,128)}, f32[4,128]{1,0:T(4,128)}, bf16[512,512]{1,0:T(8,128)(2,1)}) custom-call(f32[4096,512]{1,0:T(8,128)S(1)} %get-tuple-element.12.before, bf16[32,160,128]{2,1,0:T(8,128)(2,1)S(1)} %get-tuple-element.13.message, s32[32,128]{1,0:T(8,128)S(1)} %get-tuple-element.14.neg_asked, s32[8,128]{1,0:T(8,128)S(1)} %get-tuple-element.15.pos_asked, ...), custom_call_target="tpu_custom_call" | custom-call | tf_op jit(solution)/shard_map/finish/pallas_call | solution.py:880
